TPU v7x, 32 devices: a whole 2x2x4 slice. The times are simulated.
32 devices in a mesh: dp: 8 (over z, y), tensor: 4 (over x, core).
Axes of the slice: x: 2, y: 2, z: 4, core: 2. Of those that a mesh axis runs over, the one named last changes fastest.
Arguments:
- hidden_in: bfloat16 [8, 512, 4096], P('dp', None, 'tensor'), may hold values from -6 to 6
- norm_gain: bfloat16 [4096], replicated, may hold values from 0.25 to 1.75
- w_query: bfloat16 [4096, 4096], P('dp', 'tensor'), may hold values from -0.09375 to 0.09375
- w_key: bfloat16 [4096, 1024], P('dp', 'tensor'), may hold values from -0.09375 to 0.09375
- w_value: bfloat16 [4096, 1024], P('dp', 'tensor'), may hold values from -0.09375 to 0.09375
- w_out: bfloat16 [4096, 4096], P('tensor', 'dp'), may hold values from -0.09375 to 0.09375
- final_gain: bfloat16 [4096], P('tensor'), may hold values from 0.25 to 1.75
- latents: bfloat16 [512, 4096], P(None, 'tensor'), may hold values from -200 to 200
- token_mask: int32 [8, 512], P('dp'), may hold values from 0 to 1, as said below
- queries: bfloat16 [16384, 4096], P('dp', 'tensor'), may hold values from -6 to 6
Outputs:
- similarity_matrix: float32 [16384, 8], P('dp')
- log_norm: float32 [16384], P('dp')
Inputs may be any that keep to these rules, and one draw needn't show every extreme that they name: `token_mask`: in each passage the mask is 1 on a leading run of at least 64 tokens and 0 after it; the first passage has no padding.
All inputs are finite; a program needn't handle non-finite values.
Results may differ from a plain program's by a relative error of at most 0.015.
Values may be sent and summed in bfloat16 or wider, within the bound.
A program may use at most 128 MiB of HBM per device.

v0:
```python
import jax
import jax.numpy as jnp
from jax import lax
from jax.sharding import PartitionSpec as P

HEAD = 128


EPS = 1e-05
logit_divisor = 0.02


def apply_rotary(values, sequence_indices):
    half = values.shape[-1] // 2
    freqs = 10000.0 ** (-2.0 * jnp.arange(half, dtype=jnp.float32) / values.shape[-1])
    angle = sequence_indices[:, None] * freqs[None, :]
    cosine = jnp.cos(angle)[:, None, :]
    sine = jnp.sin(angle)[:, None, :]
    first = values[..., :half]
    second = values[..., half:]
    return jnp.concatenate(
        [first * cosine - second * sine, second * cosine + first * sine], axis=-1
    )


def local(
    hidden_in, norm_gain, w_query, w_key, w_value, w_out, final_gain, latents, token_mask, queries
):
    count_p, length, part_width = hidden_in.shape
    total_rows = count_p * length
    rows = hidden_in.reshape(total_rows, part_width)
    full = lax.all_gather(rows, "tensor", axis=1, tiled=True)
    width = full.shape[1]
    full_f = full.astype(jnp.float32)
    normed = (
        full_f
        * lax.rsqrt(jnp.mean(full_f * full_f, -1, keepdims=True) + EPS)
        * norm_gain.astype(jnp.float32)
    ).astype(jnp.bfloat16)

    def add_rows(piece):
        return jnp.dot(normed, piece, preferred_element_type=jnp.float32)

    query = add_rows(lax.all_gather(w_query, "dp", axis=0, tiled=True))
    key = add_rows(lax.all_gather(w_key, "dp", axis=0, tiled=True))
    value = add_rows(lax.all_gather(w_value, "dp", axis=0, tiled=True))
    shard_heads = query.shape[1] // HEAD
    local_kv = key.shape[1] // HEAD
    group = shard_heads // local_kv
    scale = HEAD ** (-0.5)
    sequence_indices = jnp.arange(length, dtype=jnp.float32)
    q_rot = apply_rotary(
        query.reshape(count_p, length, shard_heads, HEAD), sequence_indices
    ).astype(jnp.bfloat16)
    q_rot = q_rot.reshape(count_p, length, local_kv, group, HEAD)
    k_rot = apply_rotary(key.reshape(count_p, length, local_kv, HEAD), sequence_indices).astype(
        jnp.bfloat16
    )
    v_half = value.astype(jnp.bfloat16).reshape(count_p, length, local_kv, HEAD)
    logits = (
        jnp.einsum("pqgrd,pkgd->pgrqk", q_rot, k_rot, preferred_element_type=jnp.float32) * scale
    )
    logits = jnp.where(token_mask[:, None, None, None, :] > 0, logits, -1e30)
    attention_weights = jax.nn.softmax(logits, axis=-1).astype(jnp.bfloat16)
    attended_values = jnp.einsum(
        "pgrqk,pkgd->pqgrd", attention_weights, v_half, preferred_element_type=jnp.float32
    )
    attended_values = attended_values.astype(jnp.bfloat16).reshape(total_rows, shard_heads * HEAD)
    terms = jnp.dot(
        attended_values,
        lax.all_gather(w_out, "dp", axis=1, tiled=True),
        preferred_element_type=jnp.float32,
    )
    start = lax.axis_index("tensor") * part_width
    summed = lax.psum(terms, "tensor")
    hidden_complete = (full_f + summed).astype(jnp.bfloat16).astype(jnp.float32)
    total_sq = jnp.sum(hidden_complete * hidden_complete, -1, keepdims=True)
    h_own = lax.dynamic_slice_in_dim(hidden_complete, start, part_width, 1)
    hn = (h_own * lax.rsqrt(total_sq / width + EPS) * final_gain.astype(jnp.float32)).astype(
        jnp.bfloat16
    )
    hn_heads = hn.reshape(count_p, length, shard_heads, HEAD)
    lat_heads = latents.reshape(latents.shape[0], shard_heads, HEAD)
    cross_logits = (
        jnp.einsum("pqhd,khd->phqk", hn_heads, lat_heads, preferred_element_type=jnp.float32)
        * scale
    )
    latent_cross_weights = jax.nn.softmax(cross_logits, axis=-1).astype(jnp.bfloat16)
    cross = jnp.einsum(
        "phqk,khd->pqhd", latent_cross_weights, lat_heads, preferred_element_type=jnp.float32
    )
    mixed = hn.astype(jnp.float32).reshape(count_p, length, part_width) + cross.reshape(
        count_p, length, part_width
    )
    mask_f = token_mask.astype(jnp.float32)
    pooled = jnp.sum(mixed * mask_f[:, :, None], axis=1) / jnp.sum(mask_f, axis=1, keepdims=True)
    pooled_sq = lax.psum(jnp.sum(pooled * pooled, -1, keepdims=True), "tensor")
    embedding = (pooled * lax.rsqrt(pooled_sq + 1e-06)).astype(jnp.bfloat16)
    every = lax.all_gather(embedding, "dp", axis=0, tiled=True)
    inner_product_matrix = lax.dot_general(
        queries, every, (((1,), (1,)), ((), ())), preferred_element_type=jnp.float32
    )
    q_f = queries.astype(jnp.float32)
    question_norm_sq = jnp.sum(q_f * q_f, -1)
    inner_product_matrix, question_norm_sq = lax.psum(
        (inner_product_matrix, question_norm_sq), "tensor"
    )
    similarity_matrix = (
        inner_product_matrix * lax.rsqrt(question_norm_sq + 1e-06)[:, None] / logit_divisor
    )
    log_norm = jax.nn.logsumexp(similarity_matrix, axis=1)
    return (similarity_matrix, log_norm)


def solution(mesh):
    placed = (
        P("dp", None, "tensor"),
        P(),
        P("dp", "tensor"),
        P("dp", "tensor"),
        P("dp", "tensor"),
        P("tensor", "dp"),
        P("tensor"),
        P(None, "tensor"),
        P("dp", None),
        P("dp", "tensor"),
    )
    return jax.shard_map(
        local, mesh=mesh, in_specs=placed, out_specs=(P("dp", None), P("dp")), check_vma=False
    )
```

profile of v0, /device:TPU:0, one launch (start us, length us, event | category | flops | bytes accessed | tf_op | source)
XLA Modules:
  0.0 654.9 jit_solution(2932788704191495487)
XLA Ops:
  7.2 0.7 all-gather.16.cloned.1.call-update
  7.9 0.7 all-gather.10.cloned.1.call-update
  8.7 0.7 all-gather.8.cloned.1.call-update
  9.4 0.5 all-gather.12.cloned.1.call-update
  10.0 0.5 all-gather.14.cloned.1.call-update
  10.6 0.7 convert_element_type.72
  11.3 0.7 compare_reduce_fusion
  12.0 1.0 fusion.29
  13.0 33.8 %all-gather.16.cloned.1.call-done = bf16[1,512,4096]{2,1,0:T(8,128)(2,1)} async-done(((bf16[1,512,1024]{2,1,0:T(8,128)(2,1)}), bf16[1,512,4096]{2,1,0:T(8,128)(2,1)}) %all-gather.16.cloned.1.call-update) | async-done | bytes 4194320 | tf_op jit(solution)/shard_map/all_gather | solution.py:32
  46.8 3.1 fusion
  49.9 48.4 %all-gather.10.cloned.1.call-done = bf16[4096,256]{1,0:T(8,128)(2,1)} async-done(((bf16[512,256]{1,0:T(8,128)(2,1)}), bf16[4096,256]{1,0:T(8,128)(2,1)}) %all-gather.10.cloned.1.call-update) | async-done | bytes 2097168 | tf_op jit(solution)/shard_map/all_gather | solution.py:45
  98.2 4.4 fusion.36
  102.7 0.2 copy.37
  102.9 0.2 copy.38
  103.1 0.1 fusion.24
  103.3 44.9 %all-gather.8.cloned.1.call-done = bf16[4096,256]{1,0:T(8,128)(2,1)} async-done(((bf16[512,256]{1,0:T(8,128)(2,1)}), bf16[4096,256]{1,0:T(8,128)(2,1)}) %all-gather.8.cloned.1.call-update) | async-done | bytes 2097168 | tf_op jit(solution)/shard_map/all_gather | solution.py:46
  148.2 4.4 convolution_convert_fusion
  152.6 121.0 %all-gather.12.cloned.1.call-done = bf16[4096,1024]{1,0:T(8,128)(2,1)} async-done(((bf16[512,1024]{1,0:T(8,128)(2,1)}), bf16[4096,1024]{1,0:T(8,128)(2,1)}) %all-gather.12.cloned.1.call-update) | async-done | bytes 8388624 | tf_op jit(solution)/shard_map/all_gather | solution.py:44
  273.6 8.2 %convolution_bitcast_fusion.1 = f32[64,8,8,128]{3,1,2,0:T(8,128)S(1)} fusion(bf16[4096,1024]{1,0:T(8,128)(2,1)} %all-gather.12.cloned.1.call-done, bf16[1,512,4096]{2,1,0:T(8,128)(2,1)} %all-gather.16.cloned.1.call-done, f32[4096]{0:T(1024)S(1)} %convert_element_type.72, f32[512]{0:T(512)S(1)} %add_rsqrt_fusion.2), kind=kOutput, calls=%fused_computation.31 | convolution fusion | flops 4303355904 | bytes 14698496 | tf_op jit(solution)/shard_map/dot_general | solution.py:42
  281.9 0.5 copy.41
  282.3 0.9 subtract_convert_fusion
  283.3 0.1 copy.25
  283.5 2.2 bitcast_reduce_fusion.1
  285.6 2.0 fusion.7
  287.7 2.4 fusion.14
  290.1 109.0 %all-gather.14.cloned.1.call-done = bf16[1024,4096]{1,0:T(8,128)(2,1)} async-done(((bf16[1024,512]{1,0:T(8,128)(2,1)}), bf16[1024,4096]{1,0:T(8,128)(2,1)}) %all-gather.14.cloned.1.call-update) | async-done | bytes 8388624 | tf_op jit(solution)/shard_map/all_gather | solution.py:71
  399.1 10.1 %fusion.42 = f32[512,4096]{1,0:T(8,128)} fusion(bf16[512,1024]{0,1:T(8,128)(2,1)S(1)} %bitcast.128, bf16[1024,4096]{1,0:T(8,128)(2,1)} %all-gather.14.cloned.1.call-done), kind=kOutput, calls=%fused_computation.72 | convolution fusion | flops 4294967296 | bytes 17825792 | tf_op jit(solution)/shard_map/dot_general | solution.py:69
  409.3 0.6 copy-done.3
  409.9 0.6 copy-done.1
  410.5 0.5 copy.39
  411.0 0.6 convert_reduce_fusion
  411.6 3.8 multiply_reduce_fusion
  415.5 145.0 %all-reduce.4.cloned.1.call-done = f32[512,4096]{1,0:T(8,128)} async-done(((f32[512,4096]{1,0:T(8,128)}), f32[512,4096]{1,0:T(8,128)}) %all-reduce.4.cloned.1.call-update) | async-done | bytes 8388624 | tf_op jit(solution)/shard_map/psum | solution.py:75
  560.5 5.7 multiply_reduce_fusion.1
  566.2 1.4 bitcast_reduce_fusion
  567.6 1.4 fusion.6
  569.0 0.4 copy-done
  569.4 3.2 fusion.9
  572.6 1.9 copy.36
  574.5 2.0 multiply_reduce_fusion.2
  576.6 1.3 multiply_reduce_fusion.3
  577.8 6.7 %all-reduce = (f32[1,1]{1,0:T(1,128)}, f32[2048]{0:T(1024)S(1)}) all-reduce(f32[1,1]{1,0:T(1,128)} %bitcast.29, f32[2048]{0:T(1024)S(1)} %multiply_reduce_fusion), channel_id=1, replica_groups=mesh['dp'=8,'tensor'=4] {'tensor'}, use_global_device_ids=true, to_apply=%region_10.11 | all-reduce | flops 2049 | bytes 16392 | tf_op jit(solution)/shard_map/psum | solution.py:97
  585.2 0.7 multiply_convert_fusion.1
  585.8 26.3 %all-gather.1 = bf16[8192]{0:T(1024)(128)(2,1)S(1)} all-gather(bf16[1024]{0:T(1024)(128)(2,1)S(1)} %multiply_convert_fusion.1), channel_id=3, replica_groups=mesh['dp'=8,'tensor'=4] {'dp'}, dimensions={0}, use_global_device_ids=true | all-gather | bytes 18432 | tf_op jit(solution)/shard_map/all_gather | solution.py:99
  612.2 4.0 convolution_bitcast_fusion
  616.2 30.3 %all-reduce.6.cloned.1.call-done = f32[2048,8]{0,1:T(8,128)} async-done(((f32[2048,8]{0,1:T(8,128)}), f32[2048,8]{0,1:T(8,128)}) %all-reduce.6.cloned.1.call-update) | async-done | bytes 65552 | tf_op jit(solution)/shard_map/psum | solution.py:105
  646.5 0.9 fusion.39
  647.5 0.6 log_add_fusion
  (27 shorter events, 0.6 us)
Async XLA Ops:
  7.2 39.6 %all-gather.16.cloned.1.call-start = ((), (), s32[]{:S(2)}) async-start(), calls=%async_computation.6 | async-start | bytes 5242880 | tf_op jit(solution)/shard_map/all_gather | solution.py:32
  7.9 90.3 %all-gather.10.cloned.1.call-start = ((), (), s32[]{:S(2)}) async-start(), calls=%async_computation.1 | async-start | bytes 2359296 | tf_op jit(solution)/shard_map/all_gather | solution.py:45
  8.6 139.5 %all-gather.8.cloned.1.call-start = ((), (), s32[]{:S(2)}) async-start(), calls=%async_computation | async-start | bytes 2359296 | tf_op jit(solution)/shard_map/all_gather | solution.py:46
  9.4 264.2 %all-gather.12.cloned.1.call-start = ((), (), s32[]{:S(2)}) async-start(), calls=%async_computation.2 | async-start | bytes 9437184 | tf_op jit(solution)/shard_map/all_gather | solution.py:44
  10.0 389.1 %all-gather.14.cloned.1.call-start = ((), (), s32[]{:S(2)}) async-start(), calls=%async_computation.3 | async-start | bytes 9437184 | tf_op jit(solution)/shard_map/all_gather | solution.py:71
  10.5 549.9 %all-reduce.4.cloned.1.call-start = ((), (), s32[]{:S(2)}) async-start(), calls=%async_computation.4 | async-start | bytes 16777216 | tf_op jit(solution)/shard_map/psum | solution.py:75
  409.2 0.7 copy-start.3
  409.2 1.2 copy-start.1
  409.2 1.8 copy-start.4
  409.3 237.3 %all-reduce.6.cloned.1.call-start = ((), (), s32[]{:S(2)}) async-start(), calls=%async_computation.5 | async-start | bytes 131072 | tf_op jit(solution)/shard_map/psum | solution.py:105
  566.2 3.2 copy-start
  647.4 0.7 copy-start.2
Sparse Core Ops, SparseCore 0:
  9.6 37.1 all-gather.15
  48.9 49.2 all-gather.9
  100.4 47.7 all-gather.7
  150.1 123.4 all-gather.11
  275.5 123.5 all-gather.13
  409.4 151.0 all-reduce.3
  616.3 30.1 all-reduce.5
where the time goes:
time: 655 us
  waiting for transfers between devices  536 us (82%)
  matrix products  40.4 us (6%)
  blocking collectives  33 us (5%)
  other arithmetic  25.5 us (4%)
  between operations  15 us (2%)
    psum x1, waiting for transfers between devices, local(): summed = lax.psum(terms, 'tensor')  145 us
    all_gather x1, waiting for transfers between devices, local(): query = add_rows(lax.all_gather(w_query, 'dp', axis=0, tiled=True))  121 us
    all_gather x1, waiting for transfers between devices, local(): lax.all_gather(w_out, 'dp', axis=1, tiled=True)  109 us
    all_gather x1, waiting for transfers between devices, local(): key = add_rows(lax.all_gather(w_key, 'dp', axis=0, tiled=True))  48.4 us
    all_gather x1, waiting for transfers between devices, local(): value = add_rows(lax.all_gather(w_value, 'dp', axis=0, tiled=True))  44.9 us
    all_gather x1, waiting for transfers between devices, local(): full = lax.all_gather(rows, 'tensor', axis=1, tiled=True)  33.8 us
    psum x1, waiting for transfers between devices, local(): lax.psum((inner_product_matrix, question_norm_sq), 'tensor')  30.3 us
    all_gather x1, blocking collectives, local(): every = lax.all_gather(embedding, 'dp', axis=0, tiled=True)  26.3 us
  transfers between devices with their start and end apart: 7, of which 7 were waited for; matrix products, arithmetic and copies ran while one was open for 6% of the time, Pallas kernels for 0%

commit v1 on v0

v1 whole, which is shorter than its diff:
```python
import functools

import jax
import jax.numpy as jnp
from jax import lax
from jax.experimental import pallas as pl
from jax.experimental.pallas import tpu as pltpu
from jax.sharding import PartitionSpec as P

HEAD = 128
EPS = 1e-05
logit_divisor = 0.02
MESH = pl.DeviceIdType.MESH
NT_DIMS = (((1,), (1,)), ((), ()))


def layer_kernel(
    ndp, nt,
    hid_ref, mask_ref, wp_ref, wo_ref, gain_ref, cos_ref, sin_ref,
    h_ref,
    hidb, maskb, wbuf, wob, acc, atts, att, rss, rsr, hsum,
    hsend, hrecv, msem, ysend, wsend, wrecv, asem, osend, orecv, rsend, rrecv,
):
    nz = ndp // 2
    nb = ndp // nt
    length, cw = hid_ref.shape
    _, rows, pack = wp_ref.shape
    half_q = att.shape[2]
    heads = half_q // HEAD
    d_model = cw * nt
    me = lax.axis_index("dp")
    t = lax.axis_index("tensor")
    zi = me // 2
    y = lax.rem(me, 2)
    oy = 1 - y
    nbr = 2 * zi + oy
    left = me - 2
    right = me + 2
    core_t = t + 1 - 2 * lax.rem(t, 2)
    x_t = lax.rem(t + 2, nt)
    has_left = zi > 0
    has_right = zi < nz - 1

    def rcopy(src, dst, ss, rs, dpi, ti):
        return pltpu.make_async_remote_copy(
            src_ref=src, dst_ref=dst, send_sem=ss, recv_sem=rs,
            device_id=(dpi, ti), device_id_type=MESH,
        )

    barrier = pltpu.get_barrier_semaphore()
    pl.semaphore_signal(barrier, inc=1, device_id=(nbr, t), device_id_type=MESH)
    for d in range(1, nt):
        pl.semaphore_signal(
            barrier, inc=1, device_id=(me, lax.rem(t + d, nt)), device_id_type=MESH
        )

    @pl.when(has_left)
    def _():
        pl.semaphore_signal(barrier, inc=1, device_id=(left, t), device_id_type=MESH)

    @pl.when(has_right)
    def _():
        pl.semaphore_signal(barrier, inc=1, device_id=(right, t), device_id_type=MESH)

    pl.semaphore_wait(
        barrier, nt + has_left.astype(jnp.int32) + has_right.astype(jnp.int32)
    )

    def w_copy(direction, slot, p, src):
        target = right if direction == 0 else left
        return rcopy(
            src, wbuf.at[slot, p], wsend.at[direction, slot, p], wrecv.at[slot, p], target, t
        )

    def w_wait(slot, p):
        rcopy(
            wbuf.at[slot, p], wbuf.at[slot, p], ysend, wrecv.at[slot, p], nbr, t
        ).wait_recv()

    def w_send(slot, p, src):
        @pl.when(has_right)
        def _():
            w_copy(0, slot, p, src).start()

        @pl.when(has_left)
        def _():
            w_copy(1, slot, p, src).start()

    def h_copy(src, a, b, i, dpi, ti):
        return rcopy(src, hidb.at[a, b], hsend.at[i], hrecv.at[a, b], dpi, ti)

    def h_wait(a, b):
        h_copy(hidb.at[a, b], a, b, 0, nbr, t).wait_recv()

    y_copy = rcopy(wp_ref.at[oy], wbuf.at[zi, y], ysend, wrecv.at[zi, y], nbr, t)
    m_copy = rcopy(mask_ref, maskb.at[y], msem.at[0], msem.at[1], nbr, t)
    sends = [
        h_copy(hid_ref, y, t, 0, nbr, t),
        h_copy(hid_ref, y, t, 1, me, x_t),
        h_copy(hid_ref, y, t, 2, me, core_t),
        h_copy(hidb.at[oy, t], oy, t, 3, me, x_t),
        h_copy(hidb.at[oy, t], oy, t, 4, me, core_t),
        h_copy(hidb.at[y, x_t], y, x_t, 5, me, core_t),
        h_copy(hidb.at[oy, x_t], oy, x_t, 6, me, core_t),
    ]
    y_copy.start()
    w_send(zi, y, wp_ref.at[y])
    sends[0].start()
    sends[1].start()
    sends[2].start()
    m_copy.start()

    hidb[y, t] = hid_ref[...]
    maskb[y] = mask_ref[...]
    wbuf[zi, y] = wp_ref[y]
    wob[me] = wo_ref[...]
    acc[...] = jnp.zeros_like(acc)

    w_wait(zi, oy)
    w_send(zi, oy, wbuf.at[zi, oy])

    h_wait(oy, t)
    sends[3].start()
    sends[4].start()
    h_wait(y, x_t)
    sends[5].start()

    def o_copy(kind, z, src):
        target = (right, left, nbr)[kind]
        slot = 2 * z + y
        return rcopy(src, wob.at[slot], osend.at[kind, z], orecv.at[slot], target, t)

    o_copy(2, zi, wo_ref).start()

    def forward(s):
        lo = zi - s
        hi = zi + s

        @pl.when(lo >= 0)
        def _():
            for p in range(2):
                w_wait(lo, p)

                @pl.when(has_right)
                def _():
                    w_copy(0, lo, p, wbuf.at[lo, p]).start()

        @pl.when(hi < nz)
        def _():
            for p in range(2):
                w_wait(hi, p)

                @pl.when(has_left)
                def _():
                    w_copy(1, hi, p, wbuf.at[hi, p]).start()

    tile = 256

    def multiply(slot):
        for p in range(2):
            first = (slot * 2 + p) * rows
            block = first // cw
            off = pl.multiple_of(lax.rem(first, cw), 128)

            def step(i, carry):
                b = i // (length // tile)
                r = pl.multiple_of(lax.rem(i, length // tile) * tile, tile)
                acc[b, pl.ds(r, tile), :] += jnp.dot(
                    hidb[b, block, pl.ds(r, tile), pl.ds(off, rows)],
                    wbuf[slot, p],
                    preferred_element_type=jnp.float32,
                )
                return carry

            lax.fori_loop(0, 2 * (length // tile), step, 0)

    def multiply_pair(s):
        @pl.when(zi - s >= 0)
        def _():
            multiply(zi - s)

        @pl.when(zi + s < nz)
        def _():
            multiply(zi + s)

    forward(1)
    h_wait(oy, x_t)
    sends[6].start()
    for a, b in ((y, core_t), (oy, core_t)):
        h_wait(a, b)
    x_core = lax.rem(core_t + 2, nt)
    for a, b in ((y, x_core), (oy, x_core)):
        h_wait(a, b)
    for copy in sends:
        copy.wait_send()

    norm_rows = 64

    def normalise(i, carry):
        b = i // (length // norm_rows)
        r = pl.multiple_of(lax.rem(i, length // norm_rows) * norm_rows, norm_rows)
        total = jnp.zeros((norm_rows, 1), jnp.float32)
        for k in range(nt):
            x = hidb[b, k, pl.ds(r, norm_rows), :].astype(jnp.float32)
            total += jnp.sum(x * x, axis=-1, keepdims=True)
        factor = lax.rsqrt(total / d_model + EPS)
        for k in range(nt):
            x = hidb[b, k, pl.ds(r, norm_rows), :].astype(jnp.float32)
            g = gain_ref[:, k * cw : (k + 1) * cw].astype(jnp.float32)
            hidb[b, k, pl.ds(r, norm_rows), :] = (x * factor * g).astype(jnp.bfloat16)
        return carry

    lax.fori_loop(0, 2 * (length // norm_rows), normalise, 0)

    multiply(zi)
    multiply_pair(1)

    def later(s, carry):
        forward(s)
        multiply_pair(s)
        return carry

    lax.fori_loop(2, nz, later, 0)

    def o_send(z, src):
        @pl.when(has_right)
        def _():
            o_copy(0, z, src).start()

        @pl.when(has_left)
        def _():
            o_copy(1, z, src).start()

    o_send(zi, wo_ref)
    m_copy.wait()

    def rotate(x):
        return (x * cos_ref[...] + pltpu.roll(x, HEAD // 2, 1) * sin_ref[...]).astype(
            jnp.bfloat16
        )

    def attend(b, out):
        key = rotate(acc[b, :, half_q : half_q + HEAD])
        val = acc[b, :, half_q + HEAD : half_q + 2 * HEAD].astype(jnp.bfloat16)
        keep = maskb[b][0:1, :] > 0
        for j in range(heads):
            qr = rotate(acc[b, :, j * HEAD : (j + 1) * HEAD])
            logits = lax.dot_general(qr, key, NT_DIMS, preferred_element_type=jnp.float32)
            logits = jnp.where(keep, logits * HEAD**-0.5, -1e30)
            e = jnp.exp(logits - jnp.max(logits, axis=-1, keepdims=True))
            w = (e * (1.0 / jnp.sum(e, axis=-1, keepdims=True))).astype(jnp.bfloat16)
            o = jnp.dot(w, val, preferred_element_type=jnp.float32).astype(jnp.bfloat16)
            out[:, j * HEAD : (j + 1) * HEAD] = o

    attend(oy, atts)
    a_copy = rcopy(atts, att.at[y], asem.at[0], asem.at[1], nbr, t)
    a_copy.start()
    attend(y, att.at[y])
    a_copy.wait()

    def r_copy(c):
        owner = c // nb
        d = lax.rem(owner - t + nt, nt)
        return rcopy(
            rss.at[c], rsr.at[d - 1, lax.rem(c, nb)], rsend.at[c],
            rrecv.at[d - 1, lax.rem(c, nb)], me, owner,
        )

    def project(c):
        mine = c // nb == t

        def step(i, carry):
            r = pl.multiple_of(i * tile, tile)
            term = jnp.dot(
                att[0, pl.ds(r, tile), :], wob[c, 0:half_q, :],
                preferred_element_type=jnp.float32,
            ) + jnp.dot(
                att[1, pl.ds(r, tile), :], wob[c, half_q : 2 * half_q, :],
                preferred_element_type=jnp.float32,
            )

            @pl.when(mine)
            def _():
                hsum[lax.rem(c, nb), pl.ds(r, tile), :] = term

            @pl.when(jnp.logical_not(mine))
            def _():
                rss[c, pl.ds(r, tile), :] = term.astype(jnp.bfloat16)

            return carry

        lax.fori_loop(0, length // tile, step, 0)

        @pl.when(jnp.logical_not(mine))
        def _():
            r_copy(c).start()

    def other(z):
        @pl.when((z >= 0) & (z < nz))
        def _():
            slot = 2 * z + oy
            rcopy(
                wob.at[slot], wob.at[slot], osend.at[2, z], orecv.at[slot], nbr, t
            ).wait_recv()
            project(slot)

    def o_step(s, carry):
        lo = zi - s
        hi = zi + s

        @pl.when(lo >= 0)
        def _():
            slot = wob.at[2 * lo + y]
            o_copy(2, lo, slot).wait_recv()

            @pl.when(has_right)
            def _():
                o_copy(0, lo, slot).start()

            o_copy(2, lo, slot).start()

        @pl.when(hi < nz)
        def _():
            slot = wob.at[2 * hi + y]
            o_copy(2, hi, slot).wait_recv()

            @pl.when(has_left)
            def _():
                o_copy(1, hi, slot).start()

            o_copy(2, hi, slot).start()

        @pl.when(lo >= 0)
        def _():
            project(2 * lo + y)

        @pl.when(hi < nz)
        def _():
            project(2 * hi + y)

        @pl.when(s >= 2)
        def _():
            other(zi - s + 1)
            other(zi + s - 1)

        return carry

    project(me)
    other(zi)
    lax.fori_loop(1, nz, o_step, 0)
    other(zi - nz + 1)
    other(zi + nz - 1)

    for cb in range(nb):
        cols = slice(cb * rows, (cb + 1) * rows)
        for d in range(1, nt):
            rcopy(
                rss.at[0], rsr.at[d - 1, cb], rsend.at[0], rrecv.at[d - 1, cb], me,
                lax.rem(t + d, nt),
            ).wait_recv()
        total = hsum[cb]
        for d in range(1, nt):
            total += rsr[d - 1, cb].astype(jnp.float32)
        h_ref[:, cols] = (hid_ref[:, cols].astype(jnp.float32) + total).astype(jnp.bfloat16)

    y_copy.wait_send()

    def drain(z, carry):
        o_copy(2, z, wob.at[2 * z + y]).wait_send()

        @pl.when(has_right & (z <= zi))
        def _():
            o_copy(0, z, wob.at[2 * z + y]).wait_send()
            for p in range(2):
                w_copy(0, z, p, wbuf.at[z, p]).wait_send()

        @pl.when(has_left & (z >= zi))
        def _():
            o_copy(1, z, wob.at[2 * z + y]).wait_send()
            for p in range(2):
                w_copy(1, z, p, wbuf.at[z, p]).wait_send()

        return carry

    lax.fori_loop(0, nz, drain, 0)

    def drain_terms(c, carry):
        @pl.when(c // nb != t)
        def _():
            r_copy(c).wait_send()

        return carry

    lax.fori_loop(0, ndp, drain_terms, 0)


def layer(ndp, nt, rows, mask, wp, wo, gain, cosine, sine):
    length, cw = rows.shape
    _, depth, pack = wp.shape
    half_q = wo.shape[0] // 2
    nz, nb = ndp // 2, ndp // nt
    dma = pltpu.SemaphoreType.DMA
    bf, f32 = jnp.bfloat16, jnp.float32
    return pl.pallas_call(
        functools.partial(layer_kernel, ndp, nt),
        out_shape=jax.ShapeDtypeStruct((length, cw), bf),
        in_specs=[pl.BlockSpec(memory_space=pltpu.VMEM)] * 7,
        out_specs=pl.BlockSpec(memory_space=pltpu.VMEM),
        scratch_shapes=[
            pltpu.VMEM((2, nt, length, cw), bf),
            pltpu.VMEM((2,) + mask.shape, mask.dtype),
            pltpu.VMEM((nz, 2, depth, pack), bf),
            pltpu.VMEM((ndp,) + wo.shape, bf),
            pltpu.VMEM((2, length, pack), f32),
            pltpu.VMEM((length, half_q), bf),
            pltpu.VMEM((2, length, half_q), bf),
            pltpu.VMEM((ndp, length, wo.shape[1]), bf),
            pltpu.VMEM((nt - 1, nb, length, wo.shape[1]), bf),
            pltpu.VMEM((nb, length, wo.shape[1]), f32),
            dma((7,)),
            dma((2, nt)),
            dma((2,)),
            dma,
            dma((2, nz, 2)),
            dma((nz, 2)),
            dma((2,)),
            dma((3, nz)),
            dma((ndp,)),
            dma((ndp,)),
            dma((nt - 1, nb)),
        ],
        compiler_params=pltpu.CompilerParams(
            collective_id=0, has_side_effects=True, vmem_limit_bytes=58 * 1024 * 1024
        ),
    )(rows, mask, wp, wo, gain, cosine, sine)


def local(
    ndp, nt,
    hidden_in, norm_gain, w_query, w_key, w_value, w_out, final_gain, latents, token_mask, queries,
):
    count_p, length, part_width = hidden_in.shape
    rows = hidden_in.reshape(length, part_width)
    width = part_width * nt
    shard_heads = part_width // HEAD
    scale = HEAD ** (-0.5)

    half = HEAD // 2
    freqs = 10000.0 ** (-2.0 * jnp.arange(half, dtype=jnp.float32) / HEAD)
    angle = jnp.arange(length, dtype=jnp.float32)[:, None] * freqs[None, :]
    cosine = jnp.concatenate([jnp.cos(angle)] * 2, axis=1)
    sine = jnp.concatenate([-jnp.sin(angle), jnp.sin(angle)], axis=1)

    def halves(w):
        return w.reshape(w.shape[0], 2, w.shape[1] // 2).transpose(1, 0, 2)

    wp = jnp.concatenate([halves(w_query), halves(w_key), halves(w_value)], axis=2)
    mask8 = jnp.broadcast_to(token_mask, (8, length))
    h = layer(ndp, nt, rows, mask8, wp, w_out, norm_gain[None, :], cosine, sine)

    h_own = h.astype(jnp.float32)
    total_sq = lax.psum(jnp.sum(h_own * h_own, -1), "tensor")[:, None]
    hn = (h_own * lax.rsqrt(total_sq / width + EPS) * final_gain.astype(jnp.float32)).astype(
        jnp.bfloat16
    )
    hn_heads = hn.reshape(count_p, length, shard_heads, HEAD)
    lat_heads = latents.reshape(latents.shape[0], shard_heads, HEAD)
    cross_logits = (
        jnp.einsum("pqhd,khd->phqk", hn_heads, lat_heads, preferred_element_type=jnp.float32)
        * scale
    )
    latent_cross_weights = jax.nn.softmax(cross_logits, axis=-1).astype(jnp.bfloat16)
    cross = jnp.einsum(
        "phqk,khd->pqhd", latent_cross_weights, lat_heads, preferred_element_type=jnp.float32
    )
    mixed = hn.astype(jnp.float32).reshape(count_p, length, part_width) + cross.reshape(
        count_p, length, part_width
    )
    mask_f = token_mask.astype(jnp.float32)
    pooled = jnp.sum(mixed * mask_f[:, :, None], axis=1) / jnp.sum(mask_f, axis=1, keepdims=True)
    pooled_sq = lax.psum(jnp.sum(pooled * pooled, -1, keepdims=True), "tensor")
    embedding = (pooled * lax.rsqrt(pooled_sq + 1e-06)).astype(jnp.bfloat16)
    every = lax.all_gather(embedding, "dp", axis=0, tiled=True)
    inner_product_matrix = lax.dot_general(
        queries, every, (((1,), (1,)), ((), ())), preferred_element_type=jnp.float32
    )
    q_f = queries.astype(jnp.float32)
    question_norm_sq = jnp.sum(q_f * q_f, -1)
    inner_product_matrix, question_norm_sq = lax.psum(
        (inner_product_matrix, question_norm_sq), "tensor"
    )
    similarity_matrix = (
        inner_product_matrix * lax.rsqrt(question_norm_sq + 1e-06)[:, None] / logit_divisor
    )
    log_norm = jax.nn.logsumexp(similarity_matrix, axis=1)
    return (similarity_matrix, log_norm)


def solution(mesh):
    placed = (
        P("dp", None, "tensor"),
        P(),
        P("dp", "tensor"),
        P("dp", "tensor"),
        P("dp", "tensor"),
        P("tensor", "dp"),
        P("tensor"),
        P(None, "tensor"),
        P("dp", None),
        P("dp", "tensor"),
    )
    return jax.shard_map(
        functools.partial(local, mesh.shape["dp"], mesh.shape["tensor"]),
        mesh=mesh, in_specs=placed, out_specs=(P("dp", None), P("dp")), check_vma=False,
    )
```

time: 655 us -> 346 us (0.53)
  waiting for transfers between devices: 536 us -> 28.5 us
  Pallas kernels: 0 us -> 231 us
  matrix products: 40.4 us -> 8.64 us
  other arithmetic: 25.5 us -> 15.3 us
  blocking collectives: 33 us -> 40.8 us
    all_gather x5 -> x0, waiting for transfers between devices: 357 us -> none  [the longest x1 121 us: local(): query = add_rows(lax.all_gather(w_query, 'dp', axis=0, tiled=True))]
    pallas_call x0 -> x1, Pallas kernels: none -> 231 us  [layer(): pl.pallas_call(functools.partial(layer_kernel, ndp, nt), out_shape=jax.Sh...]
    psum x1 -> x0, waiting for transfers between devices: 145 us -> none  [local(): summed = lax.psum(terms, 'tensor')]
    dot_general x6 -> x0, matrix products: 31.8 us -> none  [the longest x3 17.1 us: add_rows(): return jnp.dot(normed, piece, preferred_element_type=jnp.float32)]
    reduce_sum x3 -> x1, other arithmetic: 10.8 us -> 1.59 us  [local(): total_sq = lax.psum(jnp.sum(h_own * h_own, -1), 'tensor')[:, None]]
    psum x0 -> x1, blocking collectives: none -> 8.24 us  [local(): total_sq = lax.psum(jnp.sum(h_own * h_own, -1), 'tensor')[:, None]]
  transfers between devices with their start and end apart: 7 -> 1, of which waited for: 7 -> 1; matrix products, arithmetic and copies ran while one was open for 6% -> 0% of each run, Pallas kernels for 0% -> 0%
where the time goes in v1:
time: 346 us; the launch traced here: 345 us
  Pallas kernels  231 us (67%)
  blocking collectives  40.8 us (12%)
  waiting for transfers between devices  28.5 us (8%)
  other arithmetic  15.3 us (4%)
  between operations  14.9 us (4%)
  matrix products  8.64 us (2%)
  local copies, waits for them, and re-layouts  6.39 us (2%)
    pallas_call x1, Pallas kernels, layer(): pl.pallas_call(functools.partial(layer_kernel, ndp, nt), out_shape=jax.Sh...  231 us
    psum x1, waiting for transfers between devices, local(): lax.psum((inner_product_matrix, question_norm_sq), 'tensor')  28.5 us
    all_gather x1, blocking collectives, local(): every = lax.all_gather(embedding, 'dp', axis=0, tiled=True)  26 us
    psum x1, blocking collectives, local(): total_sq = lax.psum(jnp.sum(h_own * h_own, -1), 'tensor')[:, None]  8.24 us
  transfers between devices with their start and end apart: 1, of which 1 were waited for; matrix products, arithmetic and copies ran while one was open for 0% of the time, Pallas kernels for 0%

profile of v1, /device:TPU:0, one launch (start us, length us, event | category | flops | bytes accessed | tf_op | source)
XLA Modules:
  0.0 345.2 jit_solution(17821121902268179696)
XLA Ops:
  7.2 0.0 copy-start.3
  7.2 0.0 copy-start.4
  7.2 0.0 all-reduce.3.cloned.1.call-start
  7.2 0.7 convert_element_type.40
  8.0 1.3 convert_reduce_fusion
  9.3 1.0 fusion.14
  10.3 0.0 copy-start.6
  10.3 1.5 copy.28
  11.8 0.5 copy.29
  12.3 0.0 copy-done.3
  12.3 0.1 copy.30
  12.5 0.0 copy-start.5
  12.5 0.2 copy.31
  12.7 0.0 copy-done.4
  12.7 0.1 copy.32
  12.8 0.2 copy.33
  13.0 0.0 copy-done.6
  13.0 0.6 broadcast_in_dim.12.gain_ref
  13.6 1.0 pad_maximum_fusion.1
  14.6 1.3 pad_maximum_fusion.wp_ref
  15.9 0.0 copy-done.5
  15.9 0.6 broadcast_in_dim.11.mask_ref
  16.5 0.0 copy-start.1
  16.5 230.6 %shard_map.113 = bf16[512,1024]{1,0:T(8,128)(2,1)} custom-call(bf16[512,1024]{1,0:T(8,128)(2,1)} %bitcast.58, s32[8,512]{1,0:T(8,128)} %broadcast_in_dim.11.mask_ref, bf16[2,512,768]{2,1,0:T(8,128)(2,1)} %pad_maximum_fusion.wp_ref, bf16[1024,512]{1,0:T(8,128)(2,1)} %wo_ref.1, bf16[1,4096]{1,0:T(2,128)(2,1)} %broadcast_in_dim.12.gain_ref, ...), custom_call_target="tpu_custom_call" | custom-call | tf_op jit(solution)/shard_map/pallas_call | solution.py:404
  247.2 0.0 copy-start
  247.2 1.6 fusion.5
  248.8 8.2 %psum.28 = f32[512]{0:T(512)S(1)} all-reduce(f32[512]{0:T(512)S(1)} %fusion.5), channel_id=1, replica_groups=mesh['dp'=8,'tensor'=4] {'tensor'}, use_global_device_ids=true, to_apply=%region_1.0 | all-reduce | flops 512 | bytes 4096 | tf_op jit(solution)/shard_map/psum | solution.py:462
  257.0 0.0 copy-done.1
  257.0 0.5 copy.41
  257.6 0.0 copy-done.7
  257.6 0.0 copy-done
  257.6 1.4 bitcast_reduce_fusion
  259.0 1.4 fusion.1
  260.4 3.2 fusion.2
  263.6 1.9 copy.40
  265.5 3.1 multiply_reduce_fusion
  268.6 0.5 multiply_reduce_fusion.1
  269.1 1.3 multiply_reduce_fusion.2
  270.3 6.6 %all-reduce = (f32[1,1]{1,0:T(1,128)}, f32[2048]{0:T(1024)S(1)}) all-reduce(f32[1,1]{1,0:T(1,128)} %bitcast.19, f32[2048]{0:T(1024)S(1)} %multiply_reduce_fusion), channel_id=1, replica_groups=mesh['dp'=8,'tensor'=4] {'tensor'}, use_global_device_ids=true, to_apply=%region_7.0 | all-reduce | flops 2049 | bytes 16392 | tf_op jit(solution)/shard_map/psum | solution.py:481
  277.6 0.7 multiply_convert_fusion
  278.3 26.0 %all-gather = bf16[8192]{0:T(1024)(128)(2,1)S(1)} all-gather(bf16[1024]{0:T(1024)(128)(2,1)S(1)} %multiply_convert_fusion), channel_id=2, replica_groups=mesh['dp'=8,'tensor'=4] {'dp'}, dimensions={0}, use_global_device_ids=true | all-gather | bytes 18432 | tf_op jit(solution)/shard_map/all_gather | solution.py:483
  304.3 4.0 %convolution_bitcast_fusion = f32[2048,8]{0,1:T(8,128)} fusion(bf16[8,1024]{1,0:T(8,128)(2,1)S(1)} %reshape.108, bf16[2048,1024]{1,0:T(8,128)(2,1)} %param.19), kind=kOutput, calls=%fused_computation.11 | convolution fusion | flops 33554432 | bytes 4276224 | tf_op jit(solution)/shard_map/dot_general | solution.py:484
  308.3 0.0 all-reduce.3.cloned.1.call-update
  308.4 28.5 %all-reduce.3.cloned.1.call-done = f32[2048,8]{0,1:T(8,128)} async-done(((f32[2048,8]{0,1:T(8,128)}), f32[2048,8]{0,1:T(8,128)}) %all-reduce.3.cloned.1.call-update) | async-done | bytes 65552 | tf_op jit(solution)/shard_map/psum | solution.py:489
  336.8 0.9 fusion.16
  337.7 0.0 copy-start.2
  337.8 0.6 log_add_fusion
  338.4 0.0 copy-done.2
  (8 shorter events, 0.1 us)
Async XLA Ops:
  7.2 5.2 %copy-start.3 = (bf16[512,256]{1,0:T(8,128)(2,1)S(1)}, bf16[512,256]{1,0:T(8,128)(2,1)}, u32[]{:S(2)}) copy-start(bf16[512,256]{1,0:T(8,128)(2,1)} %param.13) | copy-start | bytes 786436
  7.2 5.5 %copy-start.4 = (bf16[512,256]{1,0:T(8,128)(2,1)S(1)}, bf16[512,256]{1,0:T(8,128)(2,1)}, u32[]{:S(2)}) copy-start(bf16[512,256]{1,0:T(8,128)(2,1)} %param.14) | copy-start | bytes 786436
  7.2 329.6 %all-reduce.3.cloned.1.call-start = ((), (), s32[]{:S(2)}) async-start(), calls=%async_computation | async-start | bytes 131072 | tf_op jit(solution)/shard_map/psum | solution.py:489
  10.3 2.7 copy-start.6
  12.5 3.4 copy-start.5
  16.5 240.5 %copy-start.1 = (bf16[512,1024]{1,0:T(8,128)(2,1)S(1)}, bf16[512,1024]{1,0:T(8,128)(2,1)}, u32[]{:S(2)}) copy-start(bf16[512,1024]{1,0:T(8,128)(2,1)} %param.17) | copy-start | bytes 3145732
  16.5 241.0 %copy-start.7 = (bf16[1024]{0:T(1024)(128)(2,1)S(1)}, bf16[1024]{0:T(1024)(128)(2,1)}, u32[]{:S(2)}) copy-start(bf16[1024]{0:T(1024)(128)(2,1)} %param.16) | copy-start | bytes 6148
  247.2 10.4 %copy-start = (bf16[512,1024]{1,0:T(8,128)(2,1)S(1)}, bf16[512,1024]{1,0:T(8,128)(2,1)}, u32[]{:S(2)}) copy-start(bf16[512,1024]{1,0:T(8,128)(2,1)} %shard_map.113) | copy-start | bytes 3145732
  337.7 0.7 copy-start.2
Sparse Core Ops, SparseCore 0:
  308.5 28.2 all-reduce.2

commit v2 on v1

--- a/solution.py
+++ b/solution.py
@@ -2,6 +2,7 @@
 
 import jax
 import jax.numpy as jnp
+import numpy as np
 from jax import lax
 from jax.experimental import pallas as pl
 from jax.experimental.pallas import tpu as pltpu
@@ -16,15 +17,18 @@
 
 def layer_kernel(
     ndp, nt,
-    hid_ref, mask_ref, wp_ref, wo_ref, gain_ref, cos_ref, sin_ref,
-    h_ref,
-    hidb, maskb, wbuf, wob, acc, atts, att, rss, rsr, hsum,
+    hid_ref, mask_ref, wq_ref, wk_ref, wv_ref, wo_ref, gain_ref, cos_ref, sin_ref,
+    fgain_ref, lat_ref, query_ref,
+    sim_ref, norm_ref,
+    hidb, maskb, wp_ref, wbuf, wob, acc, atts, att, rss, rsr, hsum,
+    hbuf, colb, fown, frec, qbuf, qown, qrec, prow, sown, srec,
     hsend, hrecv, msem, ysend, wsend, wrecv, asem, osend, orecv, rsend, rrecv,
+    fsend, frecv, qload, qsend, qrecv, psend, precv, ssend, srecv,
 ):
     nz = ndp // 2
     nb = ndp // nt
     length, cw = hid_ref.shape
-    _, rows, pack = wp_ref.shape
+    rows = wq_ref.shape[0]
     half_q = att.shape[2]
     heads = half_q // HEAD
     d_model = cw * nt
@@ -47,24 +51,30 @@
             device_id=(dpi, ti), device_id_type=MESH,
         )
 
+    q_load = pltpu.make_async_copy(query_ref, qbuf, qload)
+    q_load.start()
+
     barrier = pltpu.get_barrier_semaphore()
-    pl.semaphore_signal(barrier, inc=1, device_id=(nbr, t), device_id_type=MESH)
+
+    def greet(d, carry):
+        pl.semaphore_signal(
+            barrier, inc=1, device_id=(lax.rem(me + d, ndp), t), device_id_type=MESH
+        )
+        return carry
+
+    lax.fori_loop(1, ndp, greet, 0)
     for d in range(1, nt):
         pl.semaphore_signal(
             barrier, inc=1, device_id=(me, lax.rem(t + d, nt)), device_id_type=MESH
         )
 
-    @pl.when(has_left)
-    def _():
-        pl.semaphore_signal(barrier, inc=1, device_id=(left, t), device_id_type=MESH)
-
-    @pl.when(has_right)
-    def _():
-        pl.semaphore_signal(barrier, inc=1, device_id=(right, t), device_id_type=MESH)
-
-    pl.semaphore_wait(
-        barrier, nt + has_left.astype(jnp.int32) + has_right.astype(jnp.int32)
-    )
+    half_k = wk_ref.shape[1] // 2
+    for p in range(2):
+        wp_ref[p, :, 0:half_q] = wq_ref[:, p * half_q : (p + 1) * half_q]
+        wp_ref[p, :, half_q : half_q + half_k] = wk_ref[:, p * half_k : (p + 1) * half_k]
+        wp_ref[p, :, half_q + half_k :] = wv_ref[:, p * half_k : (p + 1) * half_k]
+
+    pl.semaphore_wait(barrier, ndp - 1 + nt - 1)
 
     def w_copy(direction, slot, p, src):
         target = right if direction == 0 else left
@@ -105,10 +115,8 @@
     ]
     y_copy.start()
     w_send(zi, y, wp_ref.at[y])
-    sends[0].start()
     sends[1].start()
     sends[2].start()
-    m_copy.start()
 
     hidb[y, t] = hid_ref[...]
     maskb[y] = mask_ref[...]
@@ -118,19 +126,26 @@
 
     w_wait(zi, oy)
     w_send(zi, oy, wbuf.at[zi, oy])
-
-    h_wait(oy, t)
-    sends[3].start()
-    sends[4].start()
+    sends[0].start()
+    m_copy.start()
     h_wait(y, x_t)
     sends[5].start()
 
-    def o_copy(kind, z, src):
+    pieces = 4
+    depth = wo_ref.shape[0] // pieces
+
+    def o_copy(kind, z, k, own=False):
         target = (right, left, nbr)[kind]
         slot = 2 * z + y
-        return rcopy(src, wob.at[slot], osend.at[kind, z], orecv.at[slot], target, t)
-
-    o_copy(2, zi, wo_ref).start()
+        part = pl.ds(k * depth, depth)
+        src = wo_ref.at[part] if own else wob.at[slot, part]
+        return rcopy(
+            src, wob.at[slot, part], osend.at[kind, z, k], orecv.at[slot, k], target, t
+        )
+
+    def o_wait(slot, k):
+        part = wob.at[slot, pl.ds(k * depth, depth)]
+        rcopy(part, part, osend.at[2, 0, k], orecv.at[slot, k], nbr, t).wait_recv()
 
     def forward(s):
         lo = zi - s
@@ -184,8 +199,42 @@
             multiply(zi + s)
 
     forward(1)
+    h_wait(oy, t)
+    sends[3].start()
+    sends[4].start()
+    for k in range(pieces):
+        o_copy(2, zi, k, own=True).start()
+
+    ones = jnp.ones((8, cw), jnp.bfloat16)
+
+    def row_sums(x):
+        x = x.astype(jnp.float32)
+        square = x * x
+        high = square.astype(jnp.bfloat16)
+        low = (square - high.astype(jnp.float32)).astype(jnp.bfloat16)
+        return lax.dot_general(
+            ones, high, NT_DIMS, preferred_element_type=jnp.float32
+        ) + lax.dot_general(ones, low, NT_DIMS, preferred_element_type=jnp.float32)
+
+    def over_tensor(d, src, dst, ss, rs):
+        return rcopy(
+            src, dst.at[d - 1], ss.at[d - 1], rs.at[d - 1], me, lax.rem(t + d, nt)
+        )
+
+    q_load.wait()
+    count = qbuf.shape[0]
+
+    def query_norm(i, carry):
+        r = pl.multiple_of(i * 128, 128)
+        qown[:, pl.ds(r, 128)] = row_sums(qbuf[pl.ds(r, 128), :])
+        return carry
+
+    lax.fori_loop(0, count // 128, query_norm, 0)
+    q_copies = [over_tensor(d, qown, qrec, qsend, qrecv) for d in range(1, nt)]
     h_wait(oy, x_t)
     sends[6].start()
+    for copy in q_copies:
+        copy.start()
     for a, b in ((y, core_t), (oy, core_t)):
         h_wait(a, b)
     x_core = lax.rem(core_t + 2, nt)
@@ -213,25 +262,25 @@
     lax.fori_loop(0, 2 * (length // norm_rows), normalise, 0)
 
     multiply(zi)
-    multiply_pair(1)
 
     def later(s, carry):
         forward(s)
-        multiply_pair(s)
+        multiply_pair(s - 1)
         return carry
 
     lax.fori_loop(2, nz, later, 0)
 
-    def o_send(z, src):
+    for k in range(pieces):
+
         @pl.when(has_right)
         def _():
-            o_copy(0, z, src).start()
+            o_copy(0, zi, k, own=True).start()
 
         @pl.when(has_left)
         def _():
-            o_copy(1, z, src).start()
-
-    o_send(zi, wo_ref)
+            o_copy(1, zi, k, own=True).start()
+
+    multiply_pair(nz - 1)
     m_copy.wait()
 
     def rotate(x):
@@ -299,36 +348,34 @@
         @pl.when((z >= 0) & (z < nz))
         def _():
             slot = 2 * z + oy
-            rcopy(
-                wob.at[slot], wob.at[slot], osend.at[2, z], orecv.at[slot], nbr, t
-            ).wait_recv()
+            for k in range(pieces):
+                o_wait(slot, k)
             project(slot)
 
     def o_step(s, carry):
         lo = zi - s
         hi = zi + s
-
-        @pl.when(lo >= 0)
-        def _():
-            slot = wob.at[2 * lo + y]
-            o_copy(2, lo, slot).wait_recv()
-
-            @pl.when(has_right)
+        for k in range(pieces):
+
+            @pl.when(lo >= 0)
             def _():
-                o_copy(0, lo, slot).start()
-
-            o_copy(2, lo, slot).start()
-
-        @pl.when(hi < nz)
-        def _():
-            slot = wob.at[2 * hi + y]
-            o_copy(2, hi, slot).wait_recv()
-
-            @pl.when(has_left)
+                o_wait(2 * lo + y, k)
+
+                @pl.when(has_right)
+                def _():
+                    o_copy(0, lo, k).start()
+
+                o_copy(2, lo, k).start()
+
+            @pl.when(hi < nz)
             def _():
-                o_copy(1, hi, slot).start()
-
-            o_copy(2, hi, slot).start()
+                o_wait(2 * hi + y, k)
+
+                @pl.when(has_left)
+                def _():
+                    o_copy(1, hi, k).start()
+
+                o_copy(2, hi, k).start()
 
         @pl.when(lo >= 0)
         def _():
@@ -352,31 +399,140 @@
     other(zi + nz - 1)
 
     for cb in range(nb):
-        cols = slice(cb * rows, (cb + 1) * rows)
         for d in range(1, nt):
             rcopy(
                 rss.at[0], rsr.at[d - 1, cb], rsend.at[0], rrecv.at[d - 1, cb], me,
                 lax.rem(t + d, nt),
             ).wait_recv()
-        total = hsum[cb]
-        for d in range(1, nt):
-            total += rsr[d - 1, cb].astype(jnp.float32)
-        h_ref[:, cols] = (hid_ref[:, cols].astype(jnp.float32) + total).astype(jnp.bfloat16)
+
+    def add_terms(i, carry):
+        r = pl.multiple_of(i * 128, 128)
+        part = pl.ds(r, 128)
+        for cb in range(nb):
+            cols = slice(cb * rows, (cb + 1) * rows)
+            total = hsum[cb, part, :]
+            for d in range(1, nt):
+                total += rsr[d - 1, cb, part, :].astype(jnp.float32)
+            hbuf[part, cols] = (hid_ref[part, cols].astype(jnp.float32) + total).astype(
+                jnp.bfloat16
+            )
+        fown[:, part] = row_sums(hbuf[part, :])
+        return carry
+
+    lax.fori_loop(0, length // 128, add_terms, 0)
+    f_copies = [over_tensor(d, fown, frec, fsend, frecv) for d in range(1, nt)]
+    for copy in f_copies:
+        copy.start()
+    mask_row = mask_ref[...].astype(jnp.float32)
+    tokens = jnp.sum(mask_row[0:1, :], axis=1, keepdims=True)
+    mask_col = jnp.broadcast_to(mask_row[0:1, :], (128, length)).T[:, 0:1]
+    for copy in f_copies:
+        copy.wait_recv()
+    squares = fown[0:1, :]
+    for d in range(1, nt):
+        squares += frec[d - 1][0:1, :]
+    factor_row = lax.rsqrt(squares / d_model + EPS)
+    colb[...] = jnp.broadcast_to(factor_row, (128, length)).T
+
+    def final_norm(i, carry):
+        r = pl.multiple_of(i * norm_rows, norm_rows)
+        part = pl.ds(r, norm_rows)
+        x = hbuf[part, :].astype(jnp.float32)
+        g = fgain_ref[...].astype(jnp.float32)
+        hbuf[part, :] = (x * colb[part, 0:1] * g).astype(jnp.bfloat16)
+        return carry
+
+    lax.fori_loop(0, length // norm_rows, final_norm, 0)
+
+    for j in range(cw // HEAD):
+        cols = slice(j * HEAD, (j + 1) * HEAD)
+        hn = hbuf[:, cols]
+        lat = lat_ref[:, cols]
+        logits = lax.dot_general(hn, lat, NT_DIMS, preferred_element_type=jnp.float32)
+        logits = logits * HEAD**-0.5
+        e = jnp.exp(logits - jnp.max(logits, axis=-1, keepdims=True))
+        w = (e * (1.0 / jnp.sum(e, axis=-1, keepdims=True))).astype(jnp.bfloat16)
+        mixed = hn.astype(jnp.float32) + jnp.dot(w, lat, preferred_element_type=jnp.float32)
+        pooled = jnp.sum(mixed * mask_col, axis=0, keepdims=True) / tokens
+        prow[me, :, cols] = jnp.broadcast_to(pooled, (8, HEAD))
+
+    def p_copy(d):
+        return rcopy(
+            prow.at[me], prow.at[me], psend.at[d - 1], precv.at[me], lax.rem(me + d, ndp), t
+        )
+
+    def p_start(d, carry):
+        p_copy(d).start()
+        return carry
+
+    def p_wait(d, carry):
+        src = lax.rem(me + d, ndp)
+        rcopy(
+            prow.at[src], prow.at[src], psend.at[d - 1], precv.at[src], src, t
+        ).wait_recv()
+        return carry
+
+    lax.fori_loop(1, ndp, p_start, 0)
+    lax.fori_loop(1, ndp, p_wait, 0)
+    every = jnp.concatenate([prow[i, 0:1, :] for i in range(ndp)], axis=0)
+    sown[:, count:] = jnp.broadcast_to(
+        jnp.sum(every * every, axis=1, keepdims=True), (ndp, 128)
+    )
+    every = every.astype(jnp.bfloat16)
+
+    def score(i, carry):
+        r = pl.multiple_of(i * 256, 256)
+        sown[:, pl.ds(r, 256)] = lax.dot_general(
+            every, qbuf[pl.ds(r, 256), :], NT_DIMS, preferred_element_type=jnp.float32
+        )
+        return carry
+
+    lax.fori_loop(0, count // 256, score, 0)
+    s_copies = [over_tensor(d, sown, srec, ssend, srecv) for d in range(1, nt)]
+    for copy in s_copies:
+        copy.start()
+    for copy in q_copies + s_copies:
+        copy.wait_recv()
+    scores = sown[...]
+    query_sq = qown[0:1, :]
+    for d in range(1, nt):
+        scores += srec[d - 1]
+        query_sq += qrec[d - 1][0:1, :]
+    similarity = (
+        scores[:, :count]
+        * lax.rsqrt(scores[:, count : count + 1] + 1e-06)
+        * (lax.rsqrt(query_sq + 1e-06) / logit_divisor)
+    )
+    sim_ref[...] = similarity
+    top = jnp.max(similarity, axis=0, keepdims=True)
+    norm_ref[...] = top + jnp.log(jnp.sum(jnp.exp(similarity - top), axis=0, keepdims=True))
+
+    for copy in f_copies + q_copies + s_copies:
+        copy.wait_send()
+
+    def p_drain(d, carry):
+        p_copy(d).wait_send()
+        return carry
+
+    lax.fori_loop(1, ndp, p_drain, 0)
 
     y_copy.wait_send()
 
     def drain(z, carry):
-        o_copy(2, z, wob.at[2 * z + y]).wait_send()
+        for k in range(pieces):
+            o_copy(2, z, k).wait_send()
 
         @pl.when(has_right & (z <= zi))
         def _():
-            o_copy(0, z, wob.at[2 * z + y]).wait_send()
+            for k in range(pieces):
+                o_copy(0, z, k).wait_send()
             for p in range(2):
                 w_copy(0, z, p, wbuf.at[z, p]).wait_send()
 
         @pl.when(has_left & (z >= zi))
         def _():
-            o_copy(1, z, wob.at[2 * z + y]).wait_send()
+            for k in range(pieces):
+                o_copy(1, z, k).wait_send()
             for p in range(2):
                 w_copy(1, z, p, wbuf.at[z, p]).wait_send()
 
@@ -394,21 +550,28 @@
     lax.fori_loop(0, ndp, drain_terms, 0)
 
 
-def layer(ndp, nt, rows, mask, wp, wo, gain, cosine, sine):
+def layer(ndp, nt, rows, mask, wq, wk, wv, wo, gain, cosine, sine, fgain, lat, queries):
     length, cw = rows.shape
-    _, depth, pack = wp.shape
+    depth = wq.shape[0]
+    pack = (wq.shape[1] + wk.shape[1] + wv.shape[1]) // 2
     half_q = wo.shape[0] // 2
     nz, nb = ndp // 2, ndp // nt
+    count = queries.shape[0]
     dma = pltpu.SemaphoreType.DMA
     bf, f32 = jnp.bfloat16, jnp.float32
+    vmem = pl.BlockSpec(memory_space=pltpu.VMEM)
     return pl.pallas_call(
         functools.partial(layer_kernel, ndp, nt),
-        out_shape=jax.ShapeDtypeStruct((length, cw), bf),
-        in_specs=[pl.BlockSpec(memory_space=pltpu.VMEM)] * 7,
-        out_specs=pl.BlockSpec(memory_space=pltpu.VMEM),
+        out_shape=(
+            jax.ShapeDtypeStruct((ndp, count), f32),
+            jax.ShapeDtypeStruct((1, count), f32),
+        ),
+        in_specs=[vmem] * 11 + [pl.BlockSpec(memory_space=pl.ANY)],
+        out_specs=(vmem, vmem),
         scratch_shapes=[
             pltpu.VMEM((2, nt, length, cw), bf),
             pltpu.VMEM((2,) + mask.shape, mask.dtype),
+            pltpu.VMEM((2, depth, pack), bf),
             pltpu.VMEM((nz, 2, depth, pack), bf),
             pltpu.VMEM((ndp,) + wo.shape, bf),
             pltpu.VMEM((2, length, pack), f32),
@@ -417,6 +580,16 @@
             pltpu.VMEM((ndp, length, wo.shape[1]), bf),
             pltpu.VMEM((nt - 1, nb, length, wo.shape[1]), bf),
             pltpu.VMEM((nb, length, wo.shape[1]), f32),
+            pltpu.VMEM((length, cw), bf),
+            pltpu.VMEM((length, 128), f32),
+            pltpu.VMEM((8, length), f32),
+            pltpu.VMEM((nt - 1, 8, length), f32),
+            pltpu.VMEM((count, cw), bf),
+            pltpu.VMEM((8, count), f32),
+            pltpu.VMEM((nt - 1, 8, count), f32),
+            pltpu.VMEM((ndp, 8, cw), f32),
+            pltpu.VMEM((ndp, count + 128), f32),
+            pltpu.VMEM((nt - 1, ndp, count + 128), f32),
             dma((7,)),
             dma((2, nt)),
             dma((2,)),
@@ -424,76 +597,43 @@
             dma((2, nz, 2)),
             dma((nz, 2)),
             dma((2,)),
-            dma((3, nz)),
-            dma((ndp,)),
+            dma((3, nz, 4)),
+            dma((ndp, 4)),
             dma((ndp,)),
             dma((nt - 1, nb)),
+            dma((nt - 1,)),
+            dma((nt - 1,)),
+            dma,
+            dma((nt - 1,)),
+            dma((nt - 1,)),
+            dma((ndp - 1,)),
+            dma((ndp,)),
+            dma((nt - 1,)),
+            dma((nt - 1,)),
         ],
         compiler_params=pltpu.CompilerParams(
-            collective_id=0, has_side_effects=True, vmem_limit_bytes=58 * 1024 * 1024
+            collective_id=0, has_side_effects=True, vmem_limit_bytes=60 * 1024 * 1024
         ),
-    )(rows, mask, wp, wo, gain, cosine, sine)
+    )(rows, mask, wq, wk, wv, wo, gain, cosine, sine, fgain, lat, queries)
 
 
 def local(
     ndp, nt,
     hidden_in, norm_gain, w_query, w_key, w_value, w_out, final_gain, latents, token_mask, queries,
 ):
-    count_p, length, part_width = hidden_in.shape
+    _, length, part_width = hidden_in.shape
     rows = hidden_in.reshape(length, part_width)
-    width = part_width * nt
-    shard_heads = part_width // HEAD
-    scale = HEAD ** (-0.5)
-
     half = HEAD // 2
-    freqs = 10000.0 ** (-2.0 * jnp.arange(half, dtype=jnp.float32) / HEAD)
-    angle = jnp.arange(length, dtype=jnp.float32)[:, None] * freqs[None, :]
-    cosine = jnp.concatenate([jnp.cos(angle)] * 2, axis=1)
-    sine = jnp.concatenate([-jnp.sin(angle), jnp.sin(angle)], axis=1)
-
-    def halves(w):
-        return w.reshape(w.shape[0], 2, w.shape[1] // 2).transpose(1, 0, 2)
-
-    wp = jnp.concatenate([halves(w_query), halves(w_key), halves(w_value)], axis=2)
+    freqs = np.float32(10000.0) ** (-2.0 * np.arange(half, dtype=np.float32) / HEAD)
+    angle = np.arange(length, dtype=np.float32)[:, None] * freqs.astype(np.float32)[None, :]
+    cosine = jnp.asarray(np.concatenate([np.cos(angle)] * 2, axis=1), jnp.float32)
+    sine = jnp.asarray(np.concatenate([-np.sin(angle), np.sin(angle)], axis=1), jnp.float32)
     mask8 = jnp.broadcast_to(token_mask, (8, length))
-    h = layer(ndp, nt, rows, mask8, wp, w_out, norm_gain[None, :], cosine, sine)
-
-    h_own = h.astype(jnp.float32)
-    total_sq = lax.psum(jnp.sum(h_own * h_own, -1), "tensor")[:, None]
-    hn = (h_own * lax.rsqrt(total_sq / width + EPS) * final_gain.astype(jnp.float32)).astype(
-        jnp.bfloat16
+    similarity, log_norm = layer(
+        ndp, nt, rows, mask8, w_query, w_key, w_value, w_out, norm_gain[None, :], cosine, sine,
+        final_gain[None, :], latents, queries,
     )
-    hn_heads = hn.reshape(count_p, length, shard_heads, HEAD)
-    lat_heads = latents.reshape(latents.shape[0], shard_heads, HEAD)
-    cross_logits = (
-        jnp.einsum("pqhd,khd->phqk", hn_heads, lat_heads, preferred_element_type=jnp.float32)
-        * scale
-    )
-    latent_cross_weights = jax.nn.softmax(cross_logits, axis=-1).astype(jnp.bfloat16)
-    cross = jnp.einsum(
-        "phqk,khd->pqhd", latent_cross_weights, lat_heads, preferred_element_type=jnp.float32
-    )
-    mixed = hn.astype(jnp.float32).reshape(count_p, length, part_width) + cross.reshape(
-        count_p, length, part_width
-    )
-    mask_f = token_mask.astype(jnp.float32)
-    pooled = jnp.sum(mixed * mask_f[:, :, None], axis=1) / jnp.sum(mask_f, axis=1, keepdims=True)
-    pooled_sq = lax.psum(jnp.sum(pooled * pooled, -1, keepdims=True), "tensor")
-    embedding = (pooled * lax.rsqrt(pooled_sq + 1e-06)).astype(jnp.bfloat16)
-    every = lax.all_gather(embedding, "dp", axis=0, tiled=True)
-    inner_product_matrix = lax.dot_general(
-        queries, every, (((1,), (1,)), ((), ())), preferred_element_type=jnp.float32
-    )
-    q_f = queries.astype(jnp.float32)
-    question_norm_sq = jnp.sum(q_f * q_f, -1)
-    inner_product_matrix, question_norm_sq = lax.psum(
-        (inner_product_matrix, question_norm_sq), "tensor"
-    )
-    similarity_matrix = (
-        inner_product_matrix * lax.rsqrt(question_norm_sq + 1e-06)[:, None] / logit_divisor
-    )
-    log_norm = jax.nn.logsumexp(similarity_matrix, axis=1)
-    return (similarity_matrix, log_norm)
+    return similarity.T, log_norm[0]
 
 
 def solution(mesh):

time: 346 us -> 256 us (0.74)
  blocking collectives: 40.8 us -> 0 us
  waiting for transfers between devices: 28.5 us -> 0 us
  Pallas kernels: 231 us -> 248 us
  other arithmetic: 15.3 us -> 0 us
  between operations: 14.9 us -> 0.64 us
  matrix products: 8.64 us -> 0 us
    psum x1 -> x0, waiting for transfers between devices: 28.5 us -> none  [local(): lax.psum((inner_product_matrix, question_norm_sq), 'tensor')]
    all_gather x1 -> x0, blocking collectives: 26 us -> none  [local(): every = lax.all_gather(embedding, 'dp', axis=0, tiled=True)]
    pallas_call x1, Pallas kernels: 231 us -> 248 us  [layer(): pl.pallas_call(functools.partial(layer_kernel, ndp, nt), out_shape=(jax.S...]
    psum x2 -> x0, blocking collectives: 14.8 us -> none  [the longest x1 8.24 us: local(): total_sq = lax.psum(jnp.sum(h_own * h_own, -1), 'tensor')[:, None]]
    reduce_sum x7 -> x0, other arithmetic: 9.1 us -> none  [the longest x1 3.08 us: local(): question_norm_sq = jnp.sum(q_f * q_f, -1)]
    dot_general x3 -> x0, matrix products: 8.64 us -> none  [the longest x1 4.01 us: local(): lax.dot_general(queries, every, (((1,), (1,)), ((), ())), preferred_eleme...]
  transfers between devices with their start and end apart: 1 -> 0, of which waited for: 1 -> 0; matrix products, arithmetic and copies ran while one was open for 0% -> 0% of each run, Pallas kernels for 0% -> 0%
where the time goes in v2:
time: 256 us
  Pallas kernels  248 us (97%)
  local copies, waits for them, and re-layouts  6.64 us (3%)
    pallas_call x1, Pallas kernels, layer(): pl.pallas_call(functools.partial(layer_kernel, ndp, nt), out_shape=(jax.S...  248 us

profile of v2, /device:TPU:0, one launch (start us, length us, event | category | flops | bytes accessed | tf_op | source)
XLA Modules:
  0.0 255.7 jit_solution(9586436422318636667)
XLA Ops:
  0.6 1.3 broadcast_in_dim.16.fgain_ref
  1.9 1.3 broadcast_in_dim.15.gain_ref
  3.2 1.3 broadcast_in_dim.14.mask_ref
  4.5 248.4 %shard_map.131 = (f32[8,2048]{1,0:T(8,128)}, f32[1,2048]{1,0:T(1,128)}) custom-call(bf16[512,1024]{1,0:T(8,128)(2,1)} %bitcast.4, s32[8,512]{1,0:T(8,128)} %broadcast_in_dim.14.mask_ref, bf16[512,1024]{1,0:T(8,128)(2,1)} %wq_ref.1, bf16[512,256]{1,0:T(8,128)(2,1)} %wk_ref.1, bf16[512,256]{1,0:T(8,128)(2,1)} %wv_ref.1, bf16[1024,512]{1,0:T(8,128)(2,1)} %wo_ref.1, ...), custom_call_target="tpu_custom_call" | custom-call | tf_op jit(solution)/shard_map/pallas_call | solution.py:563
  252.9 1.5 copy.16
  254.4 1.3 copy.17

commit v3 on v2

--- a/solution.py
+++ b/solution.py
@@ -27,6 +27,7 @@
 ):
     nz = ndp // 2
     nb = ndp // nt
+    pieces, _, wide = wob.shape[1:]
     length, cw = hid_ref.shape
     rows = wq_ref.shape[0]
     half_q = att.shape[2]
@@ -121,7 +122,8 @@
     hidb[y, t] = hid_ref[...]
     maskb[y] = mask_ref[...]
     wbuf[zi, y] = wp_ref[y]
-    wob[me] = wo_ref[...]
+    for k in range(pieces):
+        wob[me, k] = wo_ref[:, k * wide : (k + 1) * wide]
     acc[...] = jnp.zeros_like(acc)
 
     w_wait(zi, oy)
@@ -131,38 +133,33 @@
     h_wait(y, x_t)
     sends[5].start()
 
-    pieces = 4
-    depth = wo_ref.shape[0] // pieces
-
-    def o_copy(kind, z, k, own=False):
+    def o_copy(kind, z, k):
         target = (right, left, nbr)[kind]
-        slot = 2 * z + y
-        part = pl.ds(k * depth, depth)
-        src = wo_ref.at[part] if own else wob.at[slot, part]
+        piece = wob.at[2 * z + y, k]
         return rcopy(
-            src, wob.at[slot, part], osend.at[kind, z, k], orecv.at[slot, k], target, t
+            piece, piece, osend.at[kind, z, k], orecv.at[2 * z + y, k], target, t
         )
 
     def o_wait(slot, k):
-        part = wob.at[slot, pl.ds(k * depth, depth)]
-        rcopy(part, part, osend.at[2, 0, k], orecv.at[slot, k], nbr, t).wait_recv()
+        piece = wob.at[slot, k]
+        rcopy(piece, piece, osend.at[2, 0, k], orecv.at[slot, k], nbr, t).wait_recv()
 
     def forward(s):
         lo = zi - s
         hi = zi + s
 
-        @pl.when(lo >= 0)
-        def _():
-            for p in range(2):
+        for p in range(2):
+
+            @pl.when(lo >= 0)
+            def _():
                 w_wait(lo, p)
 
                 @pl.when(has_right)
                 def _():
                     w_copy(0, lo, p, wbuf.at[lo, p]).start()
 
-        @pl.when(hi < nz)
-        def _():
-            for p in range(2):
+            @pl.when(hi < nz)
+            def _():
                 w_wait(hi, p)
 
                 @pl.when(has_left)
@@ -203,7 +200,7 @@
     sends[3].start()
     sends[4].start()
     for k in range(pieces):
-        o_copy(2, zi, k, own=True).start()
+        o_copy(2, zi, k).start()
 
     ones = jnp.ones((8, cw), jnp.bfloat16)
 
@@ -255,7 +252,7 @@
         factor = lax.rsqrt(total / d_model + EPS)
         for k in range(nt):
             x = hidb[b, k, pl.ds(r, norm_rows), :].astype(jnp.float32)
-            g = gain_ref[:, k * cw : (k + 1) * cw].astype(jnp.float32)
+            g = gain_ref[k * cw : (k + 1) * cw].astype(jnp.float32)[None, :]
             hidb[b, k, pl.ds(r, norm_rows), :] = (x * factor * g).astype(jnp.bfloat16)
         return carry
 
@@ -274,11 +271,11 @@
 
         @pl.when(has_right)
         def _():
-            o_copy(0, zi, k, own=True).start()
+            o_copy(0, zi, k).start()
 
         @pl.when(has_left)
         def _():
-            o_copy(1, zi, k, own=True).start()
+            o_copy(1, zi, k).start()
 
     multiply_pair(nz - 1)
     m_copy.wait()
@@ -291,7 +288,7 @@
     def attend(b, out):
         key = rotate(acc[b, :, half_q : half_q + HEAD])
         val = acc[b, :, half_q + HEAD : half_q + 2 * HEAD].astype(jnp.bfloat16)
-        keep = maskb[b][0:1, :] > 0
+        keep = maskb[b] > 0
         for j in range(heads):
             qr = rotate(acc[b, :, j * HEAD : (j + 1) * HEAD])
             logits = lax.dot_general(qr, key, NT_DIMS, preferred_element_type=jnp.float32)
@@ -307,112 +304,106 @@
     attend(y, att.at[y])
     a_copy.wait()
 
-    def r_copy(c):
+    def r_copy(c, k):
         owner = c // nb
         d = lax.rem(owner - t + nt, nt)
         return rcopy(
-            rss.at[c], rsr.at[d - 1, lax.rem(c, nb)], rsend.at[c],
-            rrecv.at[d - 1, lax.rem(c, nb)], me, owner,
-        )
-
-    def project(c):
+            rss.at[c, k], rsr.at[d - 1, lax.rem(c, nb), k], rsend.at[c, k],
+            rrecv.at[d - 1, lax.rem(c, nb), k], me, owner,
+        )
+
+    def project(c, k):
         mine = c // nb == t
-
-        def step(i, carry):
-            r = pl.multiple_of(i * tile, tile)
-            term = jnp.dot(
-                att[0, pl.ds(r, tile), :], wob[c, 0:half_q, :],
-                preferred_element_type=jnp.float32,
-            ) + jnp.dot(
-                att[1, pl.ds(r, tile), :], wob[c, half_q : 2 * half_q, :],
-                preferred_element_type=jnp.float32,
-            )
-
-            @pl.when(mine)
-            def _():
-                hsum[lax.rem(c, nb), pl.ds(r, tile), :] = term
-
-            @pl.when(jnp.logical_not(mine))
-            def _():
-                rss[c, pl.ds(r, tile), :] = term.astype(jnp.bfloat16)
-
-            return carry
-
-        lax.fori_loop(0, length // tile, step, 0)
+        term = jnp.dot(
+            att[0], wob[c, k, 0:half_q, :], preferred_element_type=jnp.float32
+        ) + jnp.dot(
+            att[1], wob[c, k, half_q : 2 * half_q, :], preferred_element_type=jnp.float32
+        )
+
+        @pl.when(mine)
+        def _():
+            hsum[lax.rem(c, nb), k] = term
 
         @pl.when(jnp.logical_not(mine))
         def _():
-            r_copy(c).start()
-
-    def other(z):
+            rss[c, k] = term.astype(jnp.bfloat16)
+            r_copy(c, k).start()
+
+    def other(z, k):
         @pl.when((z >= 0) & (z < nz))
         def _():
-            slot = 2 * z + oy
-            for k in range(pieces):
-                o_wait(slot, k)
-            project(slot)
-
-    def o_step(s, carry):
+            o_wait(2 * z + oy, k)
+            project(2 * z + oy, k)
+
+    def first(k, carry):
+        project(me, k)
+        other(zi, k)
+        return carry
+
+    lax.fori_loop(0, pieces, first, 0)
+
+    def o_step(i, carry):
+        s = 1 + i // pieces
+        k = lax.rem(i, pieces)
         lo = zi - s
         hi = zi + s
+
+        @pl.when(lo >= 0)
+        def _():
+            o_wait(2 * lo + y, k)
+
+            @pl.when(has_right)
+            def _():
+                o_copy(0, lo, k).start()
+
+            o_copy(2, lo, k).start()
+
+        @pl.when(hi < nz)
+        def _():
+            o_wait(2 * hi + y, k)
+
+            @pl.when(has_left)
+            def _():
+                o_copy(1, hi, k).start()
+
+            o_copy(2, hi, k).start()
+
+        @pl.when(lo >= 0)
+        def _():
+            project(2 * lo + y, k)
+
+        @pl.when(hi < nz)
+        def _():
+            project(2 * hi + y, k)
+
+        @pl.when(i > 0)
+        def _():
+            before = 1 + (i - 1) // pieces
+            other(zi - before, lax.rem(i - 1, pieces))
+            other(zi + before, lax.rem(i - 1, pieces))
+
+        return carry
+
+    lax.fori_loop(0, (nz - 1) * pieces, o_step, 0)
+    other(zi - nz + 1, pieces - 1)
+    other(zi + nz - 1, pieces - 1)
+
+    for cb in range(nb):
         for k in range(pieces):
-
-            @pl.when(lo >= 0)
-            def _():
-                o_wait(2 * lo + y, k)
-
-                @pl.when(has_right)
-                def _():
-                    o_copy(0, lo, k).start()
-
-                o_copy(2, lo, k).start()
-
-            @pl.when(hi < nz)
-            def _():
-                o_wait(2 * hi + y, k)
-
-                @pl.when(has_left)
-                def _():
-                    o_copy(1, hi, k).start()
-
-                o_copy(2, hi, k).start()
-
-        @pl.when(lo >= 0)
-        def _():
-            project(2 * lo + y)
-
-        @pl.when(hi < nz)
-        def _():
-            project(2 * hi + y)
-
-        @pl.when(s >= 2)
-        def _():
-            other(zi - s + 1)
-            other(zi + s - 1)
-
-        return carry
-
-    project(me)
-    other(zi)
-    lax.fori_loop(1, nz, o_step, 0)
-    other(zi - nz + 1)
-    other(zi + nz - 1)
-
-    for cb in range(nb):
-        for d in range(1, nt):
-            rcopy(
-                rss.at[0], rsr.at[d - 1, cb], rsend.at[0], rrecv.at[d - 1, cb], me,
-                lax.rem(t + d, nt),
-            ).wait_recv()
+            for d in range(1, nt):
+                rcopy(
+                    rss.at[0, k], rsr.at[d - 1, cb, k], rsend.at[0, k],
+                    rrecv.at[d - 1, cb, k], me, lax.rem(t + d, nt),
+                ).wait_recv()
 
     def add_terms(i, carry):
         r = pl.multiple_of(i * 128, 128)
         part = pl.ds(r, 128)
-        for cb in range(nb):
-            cols = slice(cb * rows, (cb + 1) * rows)
-            total = hsum[cb, part, :]
+        for j in range(nb * pieces):
+            cols = slice(j * wide, (j + 1) * wide)
+            total = hsum[j // pieces, j % pieces, part, :]
             for d in range(1, nt):
-                total += rsr[d - 1, cb, part, :].astype(jnp.float32)
+                total += rsr[d - 1, j // pieces, j % pieces, part, :].astype(jnp.float32)
             hbuf[part, cols] = (hid_ref[part, cols].astype(jnp.float32) + total).astype(
                 jnp.bfloat16
             )
@@ -424,8 +415,8 @@
     for copy in f_copies:
         copy.start()
     mask_row = mask_ref[...].astype(jnp.float32)
-    tokens = jnp.sum(mask_row[0:1, :], axis=1, keepdims=True)
-    mask_col = jnp.broadcast_to(mask_row[0:1, :], (128, length)).T[:, 0:1]
+    tokens = jnp.sum(mask_row, axis=1, keepdims=True)
+    mask_rows = jnp.broadcast_to(mask_row, (8, length)).astype(jnp.bfloat16)
     for copy in f_copies:
         copy.wait_recv()
     squares = fown[0:1, :]
@@ -438,7 +429,7 @@
         r = pl.multiple_of(i * norm_rows, norm_rows)
         part = pl.ds(r, norm_rows)
         x = hbuf[part, :].astype(jnp.float32)
-        g = fgain_ref[...].astype(jnp.float32)
+        g = fgain_ref[...].astype(jnp.float32)[None, :]
         hbuf[part, :] = (x * colb[part, 0:1] * g).astype(jnp.bfloat16)
         return carry
 
@@ -448,13 +439,19 @@
         cols = slice(j * HEAD, (j + 1) * HEAD)
         hn = hbuf[:, cols]
         lat = lat_ref[:, cols]
-        logits = lax.dot_general(hn, lat, NT_DIMS, preferred_element_type=jnp.float32)
+        logits = lax.dot_general(lat, hn, NT_DIMS, preferred_element_type=jnp.float32)
         logits = logits * HEAD**-0.5
-        e = jnp.exp(logits - jnp.max(logits, axis=-1, keepdims=True))
-        w = (e * (1.0 / jnp.sum(e, axis=-1, keepdims=True))).astype(jnp.bfloat16)
-        mixed = hn.astype(jnp.float32) + jnp.dot(w, lat, preferred_element_type=jnp.float32)
-        pooled = jnp.sum(mixed * mask_col, axis=0, keepdims=True) / tokens
-        prow[me, :, cols] = jnp.broadcast_to(pooled, (8, HEAD))
+        e = jnp.exp(logits - jnp.max(logits, axis=0, keepdims=True))
+        w = (e * (1.0 / jnp.sum(e, axis=0, keepdims=True))).astype(jnp.bfloat16)
+        seen = lax.dot_general(mask_rows, w, NT_DIMS, preferred_element_type=jnp.float32)
+        high = seen.astype(jnp.bfloat16)
+        low = (seen - high.astype(jnp.float32)).astype(jnp.bfloat16)
+        total = (
+            jnp.dot(mask_rows, hn, preferred_element_type=jnp.float32)
+            + jnp.dot(high, lat, preferred_element_type=jnp.float32)
+            + jnp.dot(low, lat, preferred_element_type=jnp.float32)
+        )
+        prow[me, :, cols] = total / tokens
 
     def p_copy(d):
         return rcopy(
@@ -543,7 +540,8 @@
     def drain_terms(c, carry):
         @pl.when(c // nb != t)
         def _():
-            r_copy(c).wait_send()
+            for k in range(pieces):
+                r_copy(c, k).wait_send()
 
         return carry
 
@@ -556,6 +554,8 @@
     pack = (wq.shape[1] + wk.shape[1] + wv.shape[1]) // 2
     half_q = wo.shape[0] // 2
     nz, nb = ndp // 2, ndp // nt
+    wide = 128
+    pieces = wo.shape[1] // wide
     count = queries.shape[0]
     dma = pltpu.SemaphoreType.DMA
     bf, f32 = jnp.bfloat16, jnp.float32
@@ -573,13 +573,13 @@
             pltpu.VMEM((2,) + mask.shape, mask.dtype),
             pltpu.VMEM((2, depth, pack), bf),
             pltpu.VMEM((nz, 2, depth, pack), bf),
-            pltpu.VMEM((ndp,) + wo.shape, bf),
+            pltpu.VMEM((ndp, pieces, wo.shape[0], wide), bf),
             pltpu.VMEM((2, length, pack), f32),
             pltpu.VMEM((length, half_q), bf),
             pltpu.VMEM((2, length, half_q), bf),
-            pltpu.VMEM((ndp, length, wo.shape[1]), bf),
-            pltpu.VMEM((nt - 1, nb, length, wo.shape[1]), bf),
-            pltpu.VMEM((nb, length, wo.shape[1]), f32),
+            pltpu.VMEM((ndp, pieces, length, wide), bf),
+            pltpu.VMEM((nt - 1, nb, pieces, length, wide), bf),
+            pltpu.VMEM((nb, pieces, length, wide), f32),
             pltpu.VMEM((length, cw), bf),
             pltpu.VMEM((length, 128), f32),
             pltpu.VMEM((8, length), f32),
@@ -597,10 +597,10 @@
             dma((2, nz, 2)),
             dma((nz, 2)),
             dma((2,)),
-            dma((3, nz, 4)),
-            dma((ndp, 4)),
-            dma((ndp,)),
-            dma((nt - 1, nb)),
+            dma((3, nz, pieces)),
+            dma((ndp, pieces)),
+            dma((ndp, pieces)),
+            dma((nt - 1, nb, pieces)),
             dma((nt - 1,)),
             dma((nt - 1,)),
             dma,
@@ -628,10 +628,9 @@
     angle = np.arange(length, dtype=np.float32)[:, None] * freqs.astype(np.float32)[None, :]
     cosine = jnp.asarray(np.concatenate([np.cos(angle)] * 2, axis=1), jnp.float32)
     sine = jnp.asarray(np.concatenate([-np.sin(angle), np.sin(angle)], axis=1), jnp.float32)
-    mask8 = jnp.broadcast_to(token_mask, (8, length))
     similarity, log_norm = layer(
-        ndp, nt, rows, mask8, w_query, w_key, w_value, w_out, norm_gain[None, :], cosine, sine,
-        final_gain[None, :], latents, queries,
+        ndp, nt, rows, token_mask, w_query, w_key, w_value, w_out, norm_gain, cosine, sine, final_gain,
+        latents, queries,
     )
     return similarity.T, log_norm[0]
 

time: 256 us -> 249 us (0.973)
  local copies, waits for them, and re-layouts: 6.64 us -> 2.77 us
  Pallas kernels: 248 us -> 245 us
    broadcast_in_dim x3 -> x0, local copies, waits for them, and re-layouts: 3.87 us -> none  [the longest x1 1.3 us: local(): norm_gain[None, :]]
    pallas_call x1, Pallas kernels: 248 us -> 245 us  [layer(): pl.pallas_call(functools.partial(layer_kernel, ndp, nt), out_shape=(jax.S...]
where the time goes in v3:
time: 249 us
  Pallas kernels  245 us (98%)
  local copies, waits for them, and re-layouts  2.77 us (1%)
    pallas_call x1, Pallas kernels, layer(): pl.pallas_call(functools.partial(layer_kernel, ndp, nt), out_shape=(jax.S...  245 us

profile of v3, /device:TPU:0, one launch (start us, length us, event | category | flops | bytes accessed | tf_op | source)
XLA Modules:
  0.0 248.8 jit_solution(12460538347401909699)
XLA Ops:
  0.6 245.3 %shard_map.131 = (f32[8,2048]{1,0:T(8,128)}, f32[1,2048]{1,0:T(1,128)}) custom-call(bf16[512,1024]{1,0:T(8,128)(2,1)} %bitcast.3, s32[1,512]{1,0:T(1,128)} %mask_ref.1, bf16[512,1024]{1,0:T(8,128)(2,1)} %wq_ref.1, bf16[512,256]{1,0:T(8,128)(2,1)} %wk_ref.1, bf16[512,256]{1,0:T(8,128)(2,1)} %wv_ref.1, bf16[1024,512]{1,0:T(8,128)(2,1)} %wo_ref.1, ...), custom_call_target="tpu_custom_call" | custom-call | tf_op jit(solution)/shard_map/pallas_call | solution.py:563
  246.0 1.5 copy.16
  247.5 1.3 copy.17

commit v4 on v3

--- a/solution.py
+++ b/solution.py
@@ -196,6 +196,17 @@
             multiply(zi + s)
 
     forward(1)
+
+    for k in range(pieces):
+
+        @pl.when(has_right)
+        def _():
+            o_copy(0, zi, k).start()
+
+        @pl.when(has_left)
+        def _():
+            o_copy(1, zi, k).start()
+
     h_wait(oy, t)
     sends[3].start()
     sends[4].start()
@@ -232,6 +243,8 @@
     sends[6].start()
     for copy in q_copies:
         copy.start()
+    if nz > 2:
+        forward(2)
     for a, b in ((y, core_t), (oy, core_t)):
         h_wait(a, b)
     x_core = lax.rem(core_t + 2, nt)
@@ -260,23 +273,46 @@
 
     multiply(zi)
 
+    if nz > 2:
+        multiply_pair(1)
+
+    def o_forward(s, k):
+        lo = zi - s
+        hi = zi + s
+
+        @pl.when(lo >= 0)
+        def _():
+            o_wait(2 * lo + y, k)
+
+            @pl.when(has_right)
+            def _():
+                o_copy(0, lo, k).start()
+
+            o_copy(2, lo, k).start()
+
+        @pl.when(hi < nz)
+        def _():
+            o_wait(2 * hi + y, k)
+
+            @pl.when(has_left)
+            def _():
+                o_copy(1, hi, k).start()
+
+            o_copy(2, hi, k).start()
+
+    early = max(nz - 3, 0)
+
     def later(s, carry):
+        def relay(k, inner):
+            o_forward(s - 2, k)
+            return inner
+
+        lax.fori_loop(0, pieces, relay, 0)
         forward(s)
         multiply_pair(s - 1)
         return carry
 
-    lax.fori_loop(2, nz, later, 0)
-
-    for k in range(pieces):
-
-        @pl.when(has_right)
-        def _():
-            o_copy(0, zi, k).start()
-
-        @pl.when(has_left)
-        def _():
-            o_copy(1, zi, k).start()
-
+    lax.fori_loop(3, nz, later, 0)
     multiply_pair(nz - 1)
     m_copy.wait()
 
@@ -342,41 +378,32 @@
 
     lax.fori_loop(0, pieces, first, 0)
 
+    def project_pair(s, k):
+        @pl.when(zi - s >= 0)
+        def _():
+            project(2 * (zi - s) + y, k)
+
+        @pl.when(zi + s < nz)
+        def _():
+            project(2 * (zi + s) + y, k)
+
+    def arrived(i, carry):
+        s = 1 + i // pieces
+        k = lax.rem(i, pieces)
+        project_pair(s, k)
+        other(zi - s, k)
+        other(zi + s, k)
+        return carry
+
+    lax.fori_loop(0, early * pieces, arrived, 0)
+
     def o_step(i, carry):
         s = 1 + i // pieces
         k = lax.rem(i, pieces)
-        lo = zi - s
-        hi = zi + s
-
-        @pl.when(lo >= 0)
-        def _():
-            o_wait(2 * lo + y, k)
-
-            @pl.when(has_right)
-            def _():
-                o_copy(0, lo, k).start()
-
-            o_copy(2, lo, k).start()
-
-        @pl.when(hi < nz)
-        def _():
-            o_wait(2 * hi + y, k)
-
-            @pl.when(has_left)
-            def _():
-                o_copy(1, hi, k).start()
-
-            o_copy(2, hi, k).start()
-
-        @pl.when(lo >= 0)
-        def _():
-            project(2 * lo + y, k)
-
-        @pl.when(hi < nz)
-        def _():
-            project(2 * hi + y, k)
-
-        @pl.when(i > 0)
+        o_forward(s, k)
+        project_pair(s, k)
+
+        @pl.when(i > early * pieces)
         def _():
             before = 1 + (i - 1) // pieces
             other(zi - before, lax.rem(i - 1, pieces))
@@ -384,7 +411,7 @@
 
         return carry
 
-    lax.fori_loop(0, (nz - 1) * pieces, o_step, 0)
+    lax.fori_loop(early * pieces, (nz - 1) * pieces, o_step, 0)
     other(zi - nz + 1, pieces - 1)
     other(zi + nz - 1, pieces - 1)
 

time: 249 us -> 237 us (0.952)
  Pallas kernels: 245 us -> 234 us
    pallas_call x1, Pallas kernels: 245 us -> 234 us  [layer(): pl.pallas_call(functools.partial(layer_kernel, ndp, nt), out_shape=(jax.S...]
where the time goes in v4:
time: 237 us
  Pallas kernels  234 us (99%)
  local copies, waits for them, and re-layouts  2.77 us (1%)
    pallas_call x1, Pallas kernels, layer(): pl.pallas_call(functools.partial(layer_kernel, ndp, nt), out_shape=(jax.S...  234 us

profile of v4, /device:TPU:0, one launch (start us, length us, event | category | flops | bytes accessed | tf_op | source)
XLA Modules:
  0.0 237.0 jit_solution(16972376387081067126)
XLA Ops:
  0.6 233.6 %shard_map.131 = (f32[8,2048]{1,0:T(8,128)}, f32[1,2048]{1,0:T(1,128)}) custom-call(bf16[512,1024]{1,0:T(8,128)(2,1)} %bitcast.3, s32[1,512]{1,0:T(1,128)} %mask_ref.1, bf16[512,1024]{1,0:T(8,128)(2,1)} %wq_ref.1, bf16[512,256]{1,0:T(8,128)(2,1)} %wk_ref.1, bf16[512,256]{1,0:T(8,128)(2,1)} %wv_ref.1, bf16[1024,512]{1,0:T(8,128)(2,1)} %wo_ref.1, ...), custom_call_target="tpu_custom_call" | custom-call | tf_op jit(solution)/shard_map/pallas_call | solution.py:590
  234.3 1.5 copy.16
  235.7 1.3 copy.17

commit v5 on v4

--- a/solution.py
+++ b/solution.py
@@ -323,16 +323,16 @@
 
     def attend(b, out):
         key = rotate(acc[b, :, half_q : half_q + HEAD])
-        val = acc[b, :, half_q + HEAD : half_q + 2 * HEAD].astype(jnp.bfloat16)
-        keep = maskb[b] > 0
+        val = acc[b, :, half_q + HEAD : half_q + 2 * HEAD].T.astype(jnp.bfloat16)
+        keep = jnp.broadcast_to(maskb[b].astype(jnp.float32), (128, length)).T[:, 0:1] > 0.5
         for j in range(heads):
             qr = rotate(acc[b, :, j * HEAD : (j + 1) * HEAD])
-            logits = lax.dot_general(qr, key, NT_DIMS, preferred_element_type=jnp.float32)
+            logits = lax.dot_general(key, qr, NT_DIMS, preferred_element_type=jnp.float32)
             logits = jnp.where(keep, logits * HEAD**-0.5, -1e30)
-            e = jnp.exp(logits - jnp.max(logits, axis=-1, keepdims=True))
-            w = (e * (1.0 / jnp.sum(e, axis=-1, keepdims=True))).astype(jnp.bfloat16)
-            o = jnp.dot(w, val, preferred_element_type=jnp.float32).astype(jnp.bfloat16)
-            out[:, j * HEAD : (j + 1) * HEAD] = o
+            e = jnp.exp(logits - jnp.max(logits, axis=0, keepdims=True))
+            w = (e * (1.0 / jnp.sum(e, axis=0, keepdims=True))).astype(jnp.bfloat16)
+            o = jnp.dot(val, w, preferred_element_type=jnp.float32)
+            out[:, j * HEAD : (j + 1) * HEAD] = o.T.astype(jnp.bfloat16)
 
     attend(oy, atts)
     a_copy = rcopy(atts, att.at[y], asem.at[0], asem.at[1], nbr, t)

time: 237 us -> 236 us (level)
  no operation moved by 1% of the time
where the time goes in v5:
time: 236 us
  Pallas kernels  233 us (99%)
  local copies, waits for them, and re-layouts  2.77 us (1%)
    pallas_call x1, Pallas kernels, layer(): pl.pallas_call(functools.partial(layer_kernel, ndp, nt), out_shape=(jax.S...  233 us

profile of v5, /device:TPU:0, one launch (start us, length us, event | category | flops | bytes accessed | tf_op | source)
XLA Modules:
  0.0 235.9 jit_solution(11053054644679536768)
XLA Ops:
  0.6 232.5 %shard_map.131 = (f32[8,2048]{1,0:T(8,128)}, f32[1,2048]{1,0:T(1,128)}) custom-call(bf16[512,1024]{1,0:T(8,128)(2,1)} %bitcast.3, s32[1,512]{1,0:T(1,128)} %mask_ref.1, bf16[512,1024]{1,0:T(8,128)(2,1)} %wq_ref.1, bf16[512,256]{1,0:T(8,128)(2,1)} %wk_ref.1, bf16[512,256]{1,0:T(8,128)(2,1)} %wv_ref.1, bf16[1024,512]{1,0:T(8,128)(2,1)} %wo_ref.1, ...), custom_call_target="tpu_custom_call" | custom-call | tf_op jit(solution)/shard_map/pallas_call | solution.py:590
  233.2 1.5 copy.16
  234.7 1.3 copy.17
